TPU v7x, 32 devices: a whole 2x2x4 slice. The times are simulated.
32 devices in a mesh: cell: 8 (over z, y), view: 4 (over x, core).
Axes of the slice: x: 2, y: 2, z: 4, core: 2. Of those that a mesh axis runs over, the one named last changes fastest.
Arguments:
- gaussians: float32 [128, 9, 256], P('cell'), as said below
- seg_count: int32 [4, 8], P('view', 'cell'), may hold values from 1 to 3, as said below
- seg_block: int32 [4, 8, 3], P('view', 'cell'), may hold values from 0 to 127, as said below
- ray_count: int32 [4, 8], P('view', 'cell'), may hold values from 576 to 2304
- camera_shift: float32 [4, 2], P('view'), may hold values from -6 to 6
- target: float32 [4, 8, 3, 2304], P('view', 'cell'), may hold values from 0 to 1
Outputs:
- image: float32 [4, 8, 3, 2304], P('view', 'cell')
- gauss_grad: float32 [128, 9, 256], P('cell')
Inputs may be any that keep to these rules, and one draw needn't show every extreme that they name: `gaussians`: each column of a block is one Gaussian: a mean, the entries a, b, c of a positive definite inverse covariance, an opacity in (0, 1), three colours. `seg_count`: tiles 2m and 2m + 1 of a view hold 4 segments together; in every view some tile holds 3. Segment k of tile t uses a block stored in cell seg_block // 16, which is t + e modulo 8 for some e from -2 to 2; entries at k >= seg_count are not used.
All inputs are finite; a program needn't handle non-finite values.
Results may differ from a plain program's by a relative error of at most 0.0003.
Values sent between devices are 32-bit elements; how exact they have to be, the bound alone decides.
A program may use at most 64 MiB of HBM per device.

v0:
```python
import jax
import jax.numpy as jnp
from jax import lax
from jax.sharding import PartitionSpec as P

TILE = 48
REACH = 2


precise = lax.Precision.HIGHEST


def shifted(block, axis, distance):
    devices = range(lax.axis_size(axis))
    route = [((i - distance) % len(devices), i) for i in devices]
    return lax.ppermute(block, axis, route)


def partner(value, axis, distance):
    mask = 2**distance
    pairs = [(source, source ^ mask) for source in range(lax.axis_size(axis))]
    return lax.ppermute(value, axis, pairs)


def pixel_frame(shift, pixels):
    pixel_ids = jnp.arange(pixels)
    centre = (TILE - 1) / 2.0
    pix_x = (pixel_ids % TILE).astype(jnp.float32) - centre - shift[0]
    pix_y = (pixel_ids // TILE).astype(jnp.float32) - centre - shift[1]
    return (pix_x, pix_y)


def triangles(length):
    row_ids = lax.broadcasted_iota(jnp.int32, (length, length), 0)
    col_ids = lax.broadcasted_iota(jnp.int32, (length, length), 1)
    return ((col_ids < row_ids).astype(jnp.float32), (col_ids > row_ids).astype(jnp.float32))


def splat(params, pix_x, pix_y):
    delta_x = pix_x[None, :] - params[0][:, None]
    delta_y = pix_y[None, :] - params[1][:, None]
    quad_form = (
        params[2][:, None] * delta_x * delta_x
        + 2.0 * params[3][:, None] * delta_x * delta_y
        + params[4][:, None] * delta_y * delta_y
    )
    alphas = params[5][:, None] * jnp.exp(-0.5 * quad_form)
    return (alphas, jnp.log1p(-alphas))


def forward_task(params, pix_x, pix_y, lower_tri):
    alphas, log_trans = splat(params, pix_x, pix_y)
    prefix = jnp.dot(lower_tri, log_trans, precision=precise, preferred_element_type=jnp.float32)
    weights = alphas * jnp.exp(prefix)
    colour = jnp.dot(params[6:9], weights, precision=precise, preferred_element_type=jnp.float32)
    totals = jnp.sum(log_trans, axis=0)
    return jnp.concatenate([colour, totals[None, :]], axis=0)


def gradient_rows(params, pix_x, pix_y, weighted, weights, weight_cot):
    features = jnp.stack(
        [jnp.ones_like(pix_x), pix_x, pix_y, pix_x * pix_x, pix_x * pix_y, pix_y * pix_y]
    )
    moments = lax.dot_general(
        features,
        weighted,
        (((1,), (1,)), ((), ())),
        precision=precise,
        preferred_element_type=jnp.float32,
    )
    colour_grad = lax.dot_general(
        weight_cot,
        weights,
        (((1,), (1,)), ((), ())),
        precision=precise,
        preferred_element_type=jnp.float32,
    )
    mean_x, mean_y, conic_a, conic_b, conic_c, opacity = (
        params[0],
        params[1],
        params[2],
        params[3],
        params[4],
        params[5],
    )
    moment_zero = moments[0]
    along_x = moments[1] - mean_x * moment_zero
    along_y = moments[2] - mean_y * moment_zero
    square_x = moments[3] - 2.0 * mean_x * moments[1] + mean_x * mean_x * moment_zero
    cross_xy = (
        moments[4] - mean_x * moments[2] - mean_y * moments[1] + mean_x * mean_y * moment_zero
    )
    square_y = moments[5] - 2.0 * mean_y * moments[2] + mean_y * mean_y * moment_zero
    grad_rows = jnp.stack(
        [
            conic_a * along_x + conic_b * along_y,
            conic_b * along_x + conic_c * along_y,
            -0.5 * square_x,
            -cross_xy,
            -0.5 * square_y,
            moment_zero / opacity,
        ]
    )
    return jnp.concatenate([grad_rows, colour_grad], axis=0)


def backward_task(params, cotangent, pix_x, pix_y, lower_tri, upper_tri):
    alphas, log_trans = splat(params, pix_x, pix_y)
    transmit = jnp.exp(
        jnp.dot(lower_tri, log_trans, precision=precise, preferred_element_type=jnp.float32)
    )
    weights = alphas * transmit
    weight_cot = cotangent[:3]
    shaded = lax.dot_general(
        params[6:9],
        weight_cot,
        (((0,), (0,)), ((), ())),
        precision=precise,
        preferred_element_type=jnp.float32,
    )
    later_sum = jnp.dot(
        upper_tri, weights * shaded, precision=precise, preferred_element_type=jnp.float32
    )
    dalpha = transmit * shaded - (later_sum + cotangent[3][None, :]) / (1.0 - alphas)
    return gradient_rows(params, pix_x, pix_y, dalpha * alphas, weights, weight_cot)


def composite(partials, live_mask, target_tile, valid_slot):
    slot_total = partials.shape[0]
    running = jnp.zeros(partials.shape[2:], jnp.float32)
    transmit = []
    for slot_index in range(slot_total):
        transmit.append(jnp.exp(running))
        running = running + partials[slot_index, 3]
    transmit = jnp.stack(transmit)
    shaded = transmit[:, None, :] * partials[:, :3]
    rendered = jnp.sum(shaded, axis=0) * live_mask
    residual = (rendered - target_tile) * live_mask
    behind = []
    running_sum = jnp.zeros_like(rendered)
    for slot_index in range(slot_total - 1, -1, -1):
        behind.insert(0, running_sum)
        running_sum = running_sum + shaded[slot_index]
    behind = jnp.stack(behind)
    valid_weight = valid_slot.astype(jnp.float32)
    weight_cot = transmit[:, None, :] * residual[None] * valid_weight[:, None, None]
    after_cot = jnp.sum(residual[None] * behind, axis=1) * valid_weight[:, None]
    return (rendered, jnp.concatenate([weight_cot, after_cot[:, None, :]], axis=1))


def shards(gaussians, seg_count, seg_block, ray_count, camera_shift, target):
    cell_count = lax.axis_size("cell")
    cell_index = lax.axis_index("cell")
    per_block = gaussians.shape[0]
    pixels = target.shape[3]
    lower_tri, upper_tri = triangles(gaussians.shape[2])
    blocks = seg_block[0, 0]
    slot_count = blocks.shape[0]
    own_count = seg_count[0, 0]
    home_cell = blocks // per_block
    local_block = blocks % per_block
    offset = (home_cell - cell_index + REACH) % cell_count - REACH
    pix_x, pix_y = pixel_frame(camera_shift[0], pixels)
    valid_slot = jnp.arange(slot_count) < own_count
    valid_weight = valid_slot.astype(jnp.float32)

    def run_forward(params):
        return forward_task(params, pix_x, pix_y, lower_tri)

    def run_backward(bundle):
        return backward_task(bundle[0], bundle[1], pix_x, pix_y, lower_tri, upper_tri)

    near_list = []
    for shift_by in range(-REACH, REACH + 1):
        if shift_by == 0:
            near_list.append(gaussians)
        else:
            near_list.append(shifted(gaussians, "cell", -shift_by))
    near_stack = jnp.concatenate(near_list, axis=0)
    pick_index = (offset + REACH) * per_block + local_block
    own_params = jnp.take(near_stack, pick_index, axis=0)
    exec_count = (slot_count + 2) // 2
    parity = cell_index % 2
    other_count = slot_count + 1 - own_count
    first_count = jnp.where(parity == 0, own_count, other_count)

    def pair_order(mine, theirs):
        return jnp.concatenate(
            [jnp.where(parity == 0, mine, theirs), jnp.where(parity == 0, theirs, mine)], axis=0
        )

    other_params = partner(own_params, "cell", 0)
    task_index = jnp.arange(exec_count) + parity * exec_count
    take_index = jnp.where(
        task_index < first_count, task_index, slot_count + task_index - first_count
    )
    take_index = jnp.clip(take_index, 0, 2 * slot_count - 1)
    live_task = (task_index < slot_count + 1).astype(jnp.float32)
    exec_params = jnp.take(pair_order(own_params, other_params), take_index, axis=0)
    exec_partials = lax.map(run_forward, exec_params)
    other_partials = partner(exec_partials, "cell", 0)
    own_task = jnp.clip(jnp.arange(slot_count) + parity * first_count, 0, 2 * exec_count - 1)
    partials = jnp.take(pair_order(exec_partials, other_partials), own_task, axis=0)
    partials = jnp.where(valid_slot[:, None, None], partials, 0.0)
    live_mask = (jnp.arange(pixels) < ray_count[0, 0]).astype(jnp.float32)
    rendered, cotangent = composite(partials, live_mask, target[0, 0], valid_slot)
    other_cot = partner(cotangent, "cell", 0)
    exec_cot = (
        jnp.take(pair_order(cotangent, other_cot), take_index, axis=0) * live_task[:, None, None]
    )
    exec_grads = lax.map(run_backward, (exec_params, exec_cot))
    other_grads = partner(exec_grads, "cell", 0)
    own_grads = (
        jnp.take(pair_order(exec_grads, other_grads), own_task, axis=0)
        * valid_weight[:, None, None]
    )
    spot_count = (2 * REACH + 1) * per_block
    onehot = (pick_index[:, None] == jnp.arange(spot_count)[None, :]).astype(jnp.float32)
    spread = jnp.einsum("sk,sjg->kjg", onehot, own_grads, precision=precise)
    spread = spread.reshape((2 * REACH + 1, per_block) + gaussians.shape[1:])
    block_grads = spread[REACH]
    for shift_by in range(-REACH, REACH + 1):
        if shift_by != 0:
            block_grads = block_grads + shifted(spread[shift_by + REACH], "cell", shift_by)
    gauss_grad = lax.psum(block_grads, "view")
    return (rendered[None, None], gauss_grad)


def solution(mesh):
    placed = (
        P("cell", None, None),
        P("view", "cell"),
        P("view", "cell", None),
        P("view", "cell"),
        P("view", None),
        P("view", "cell", None, None),
    )
    return jax.shard_map(
        shards,
        mesh=mesh,
        in_specs=placed,
        out_specs=(P("view", "cell", None, None), P("cell", None, None)),
        check_vma=False,
    )
```

profile of v0, /device:TPU:0, one launch (start us, length us, event | category | flops | bytes accessed | tf_op | source)
XLA Modules:
  0.0 163.9 jit_solution(352240247829406183)
XLA Ops:
  8.2 3.1 %collective-permute-start = (f32[16,9,256]{2,1,0:T(8,128)S(1)}, f32[16,9,256]{2,1,0:T(8,128)S(1)}, u32[]{:S(2)}, u32[]{:S(2)}) collective-permute-start(f32[16,9,256]{2,1,0:T(8,128)S(1)} %copy.22), channel_id=1, source_target_pairs={{24,0},{28,4},{0,8},{4,12},{8,16},{12,20},{16,24},{20,28},{25,1},{... | collective-permute-start | bytes 442376 | tf_op jit(solution)/shard_map/ppermute | solution.py:16
  12.8 3.2 %collective-permute-start.2 = (f32[16,9,256]{2,1,0:T(8,128)S(1)}, f32[16,9,256]{2,1,0:T(8,128)S(1)}, u32[]{:S(2)}, u32[]{:S(2)}) collective-permute-start(f32[16,9,256]{2,1,0:T(8,128)S(1)} %copy.22), channel_id=1, source_target_pairs={{4,0},{8,4},{12,8},{16,12},{20,16},{24,20},{28,24},{0,28},{5,1},{9... | collective-permute-start | bytes 442376 | tf_op jit(solution)/shard_map/ppermute | solution.py:16
  20.5 6.8 %collective-permute-done.1 = f32[16,9,256]{2,1,0:T(8,128)S(1)} collective-permute-done((f32[16,9,256]{2,1,0:T(8,128)S(1)}, f32[16,9,256]{2,1,0:T(8,128)S(1)}, u32[]{:S(2)}, u32[]{:S(2)}) %collective-permute-start.1) | collective-permute-done | bytes 147488 | tf_op jit(solution)/shard_map/ppermute | solution.py:16
  28.4 2.5 %collective-permute-done.3 = f32[16,9,256]{2,1,0:T(8,128)S(1)} collective-permute-done((f32[16,9,256]{2,1,0:T(8,128)S(1)}, f32[16,9,256]{2,1,0:T(8,128)S(1)}, u32[]{:S(2)}, u32[]{:S(2)}) %collective-permute-start.3) | collective-permute-done | bytes 147488 | tf_op jit(solution)/shard_map/ppermute | solution.py:16
  33.1 2.5 %collective-permute-done.4 = f32[3,9,256]{2,1,0:T(8,128)S(1)} collective-permute-done((f32[3,9,256]{2,1,0:T(8,128)S(1)}, f32[3,9,256]{2,1,0:T(8,128)S(1)}, u32[]{:S(2)}, u32[]{:S(2)}) %collective-permute-start.4) | collective-permute-done | bytes 27680 | tf_op jit(solution)/shard_map/ppermute | solution.py:22
  36.3 20.9 %while.24 = (s32[]{:T(128)}, f32[2,4,2304]{2,1,0:T(4,128)S(1)}, f32[2,9,256]{2,1,0:T(8,128)S(1)}, f32[]{:T(128)}, f32[]{:T(128)}, /*index=5*/s32[]{:T(128)}, s32...) while((s32[]{:T(128)}, f32[2,4,2304]{2,1,0:T(4,128)S(1)}, f32[2,9,256]{2,1,0:T(8,128)S(1)}, ...), condition=%wide.region_2.3_spmd.clone, body=%wide.region_0.2_spmd.clone.sunk | while | flops 1856945664 | bytes 4941041 | solution.py:200
  37.6 4.8 %fusion.168 = f32[256,2304]{0,1:T(8,128)S(1)} fusion(f32[256]{0:T(256)S(1)} %bitcast.268, f32[256]{0:T(256)S(1)} %bitcast.260, f32[2304]{0:T(1024)S(1)} %get-tuple-element.360, f32[256]{0:T(256)S(1)} %bitcast.262, f32[256]{0:T(256)S(1)} %bitcast.264, f32[2304]{0:T(1024)S(1)} %get-tuple-element.363, f32[256]{0:T(256)S(1)} %bitcast.266, ...), kind=kOutput, calls=%fused_computation.23.clone.1 | convolution fusion | flops 1827405824 | bytes 2383872 | tf_op jit(solution)/shard_map/while/body/eval_jaxpr/dot_general | solution.py:53
  44.4 2.3 %fusion.167 = f32[2304]{0:T(1024)S(1)} fusion(f32[256]{0:T(256)S(1)} %bitcast.269, f32[256]{0:T(256)S(1)} %bitcast.261, f32[2304]{0:T(1024)S(1)} %get-tuple-element.360, f32[256]{0:T(256)S(1)} %bitcast.263, f32[256]{0:T(256)S(1)} %bitcast.265, f32[2304]{0:T(1024)S(1)} %get-tuple-element.363, f32[256]{0:T(256)S(1)} %bitcast.267, f32[256]{0:T(256)S(1)} %bitcast.259), kind=kLoop, calls=%fused_computation.30.clone.1 | loop fusion | flops 8255232 | bytes 33792 | tf_op jit(solution)/shard_map/while/body/eval_jaxpr/reduce_sum | solution.py:56
  48.0 4.8 %fusion.168 = f32[256,2304]{0,1:T(8,128)S(1)} fusion(f32[256]{0:T(256)S(1)} %bitcast.268, f32[256]{0:T(256)S(1)} %bitcast.260, f32[2304]{0:T(1024)S(1)} %get-tuple-element.360, f32[256]{0:T(256)S(1)} %bitcast.262, f32[256]{0:T(256)S(1)} %bitcast.264, f32[2304]{0:T(1024)S(1)} %get-tuple-element.363, f32[256]{0:T(256)S(1)} %bitcast.266, ...), kind=kOutput, calls=%fused_computation.23.clone.1 | convolution fusion | flops 1827405824 | bytes 2383872 | tf_op jit(solution)/shard_map/while/body/eval_jaxpr/dot_general | solution.py:53
  54.8 2.3 %fusion.167 = f32[2304]{0:T(1024)S(1)} fusion(f32[256]{0:T(256)S(1)} %bitcast.269, f32[256]{0:T(256)S(1)} %bitcast.261, f32[2304]{0:T(1024)S(1)} %get-tuple-element.360, f32[256]{0:T(256)S(1)} %bitcast.263, f32[256]{0:T(256)S(1)} %bitcast.265, f32[2304]{0:T(1024)S(1)} %get-tuple-element.363, f32[256]{0:T(256)S(1)} %bitcast.267, f32[256]{0:T(256)S(1)} %bitcast.259), kind=kLoop, calls=%fused_computation.30.clone.1 | loop fusion | flops 8255232 | bytes 33792 | tf_op jit(solution)/shard_map/while/body/eval_jaxpr/reduce_sum | solution.py:56
  58.8 2.8 %collective-permute-done.5 = f32[2,4,2304]{2,1,0:T(4,128)S(1)} collective-permute-done((f32[2,4,2304]{2,1,0:T(4,128)S(1)}, f32[2,4,2304]{2,1,0:T(4,128)S(1)}, u32[]{:S(2)}, u32[]{:S(2)}) %collective-permute-start.5) | collective-permute-done | bytes 73760 | tf_op jit(solution)/shard_map/ppermute | solution.py:22
  64.5 3.2 %collective-permute-done.6 = f32[3,4,2304]{2,1,0:T(4,128)S(1)} collective-permute-done((f32[3,4,2304]{2,1,0:T(4,128)S(1)}, f32[3,4,2304]{2,1,0:T(4,128)S(1)}, u32[]{:S(2)}, u32[]{:S(2)}) %collective-permute-start.6) | collective-permute-done | bytes 110624 | tf_op jit(solution)/shard_map/ppermute | solution.py:22
  68.6 38.2 %while.25 = (s32[]{:T(128)}, f32[2,9,256]{2,1,0:T(8,128)S(1)}, f32[2,9,256]{2,1,0:T(8,128)S(1)}, f32[2,4,2304]{2,1,0:T(4,128)S(1)}, f32[]{:T(128)}, /*index=5*/f...) while((s32[]{:T(128)}, f32[2,9,256]{2,1,0:T(8,128)S(1)}, ...), condition=%wide.region_6.7_spmd.clone.clone, body=%wide.region_5.6_spmd.clone.clone.sunk | while | flops 3743404544 | bytes 35930456 | solution.py:211
  70.0 4.9 %fusion.182 = f32[256,2304]{0,1:T(8,128)} fusion(f32[256]{0:T(256)S(1)} %bitcast.247, f32[256]{0:T(256)S(1)} %bitcast.238, f32[2304]{0:T(1024)S(1)} %get-tuple-element.374, f32[256]{0:T(256)S(1)} %bitcast.255, f32[256]{0:T(256)S(1)} %bitcast.241, f32[2304]{0:T(1024)S(1)} %get-tuple-element.373, f32[256]{0:T(256)S(1)} %bitcast.250, f32[256]{0:T(256)S(1)} %bitcast.244), kind=kOutput, calls=%fused_computation.70.clone.1 | convolution fusion | flops 1819738112 | bytes 2383872 | tf_op jit(solution)/shard_map/while/body/eval_jaxpr/dot_general | solution.py:110
  75.0 2.1 %fusion.181 = f32[256,2304]{0,1:T(8,128)S(1)} fusion(f32[2,4,2304]{2,1,0:T(4,128)S(1)} %get-tuple-element.460, s32[]{:T(128)} %get-tuple-element.442, f32[2,9,256]{2,1,0:T(8,128)S(1)} %get-tuple-element.459, s32[]{:T(128)S(6)} %add.709), kind=kOutput, calls=%fused_computation.92.clone.1 | convolution fusion | flops 21233664 | bytes 2401284 | tf_op jit(solution)/shard_map/while/body/eval_jaxpr/dot_general | solution.py:114
  77.1 4.5 %fusion.183 = f32[256,2304]{0,1:T(8,128)S(1)} fusion(f32[256,2304]{0,1:T(8,128)S(1)} %fusion.181, f32[256,2304]{0,1:T(8,128)S(1)} %copy-done.1, f32[2304]{0:T(1024)S(1)} %dynamic-slice_reduce_fusion.2, f32[256]{0:T(256)S(1)} %bitcast.248, f32[256]{0:T(256)S(1)} %bitcast.239, f32[2304]{0:T(1024)S(1)} %get-tuple-element.374, f32[256]{0:T(256)S(1)} %bitcast.256, ...), kind=kOutput, calls=%fused_computation.74.clone.1 | convolution fusion | flops 1830944768 | bytes 7111680 | tf_op jit(solution)/shard_map/while/body/eval_jaxpr/dot_general | solution.py:121
  85.4 2.2 %fusion.186 = f32[3,256]{1,0:T(4,128)S(1)} fusion(f32[256,2304]{0,1:T(8,128)S(1)} %copy-done.2, f32[256]{0:T(256)S(1)} %bitcast.249, f32[256]{0:T(256)S(1)} %bitcast.240, f32[2304]{0:T(1024)S(1)} %get-tuple-element.374, f32[256]{0:T(256)S(1)} %bitcast.257, f32[256]{0:T(256)S(1)} %bitcast.243, f32[2304]{0:T(1024)S(1)} %get-tuple-element.373, ...), kind=kOutput, calls=%fused_computation.84.clone.1 | convolution fusion | flops 28901376 | bytes 2429956 | tf_op jit(solution)/shard_map/while/body/eval_jaxpr/dot_general | solution.py:71
  89.0 4.9 %fusion.182 = f32[256,2304]{0,1:T(8,128)} fusion(f32[256]{0:T(256)S(1)} %bitcast.247, f32[256]{0:T(256)S(1)} %bitcast.238, f32[2304]{0:T(1024)S(1)} %get-tuple-element.374, f32[256]{0:T(256)S(1)} %bitcast.255, f32[256]{0:T(256)S(1)} %bitcast.241, f32[2304]{0:T(1024)S(1)} %get-tuple-element.373, f32[256]{0:T(256)S(1)} %bitcast.250, f32[256]{0:T(256)S(1)} %bitcast.244), kind=kOutput, calls=%fused_computation.70.clone.1 | convolution fusion | flops 1819738112 | bytes 2383872 | tf_op jit(solution)/shard_map/while/body/eval_jaxpr/dot_general | solution.py:110
  94.0 2.1 %fusion.181 = f32[256,2304]{0,1:T(8,128)S(1)} fusion(f32[2,4,2304]{2,1,0:T(4,128)S(1)} %get-tuple-element.460, s32[]{:T(128)} %get-tuple-element.442, f32[2,9,256]{2,1,0:T(8,128)S(1)} %get-tuple-element.459, s32[]{:T(128)S(6)} %add.709), kind=kOutput, calls=%fused_computation.92.clone.1 | convolution fusion | flops 21233664 | bytes 2401284 | tf_op jit(solution)/shard_map/while/body/eval_jaxpr/dot_general | solution.py:114
  96.1 4.5 %fusion.183 = f32[256,2304]{0,1:T(8,128)S(1)} fusion(f32[256,2304]{0,1:T(8,128)S(1)} %fusion.181, f32[256,2304]{0,1:T(8,128)S(1)} %copy-done.1, f32[2304]{0:T(1024)S(1)} %dynamic-slice_reduce_fusion.2, f32[256]{0:T(256)S(1)} %bitcast.248, f32[256]{0:T(256)S(1)} %bitcast.239, f32[2304]{0:T(1024)S(1)} %get-tuple-element.374, f32[256]{0:T(256)S(1)} %bitcast.256, ...), kind=kOutput, calls=%fused_computation.74.clone.1 | convolution fusion | flops 1830944768 | bytes 7111680 | tf_op jit(solution)/shard_map/while/body/eval_jaxpr/dot_general | solution.py:121
  104.4 2.2 %fusion.186 = f32[3,256]{1,0:T(4,128)S(1)} fusion(f32[256,2304]{0,1:T(8,128)S(1)} %copy-done.2, f32[256]{0:T(256)S(1)} %bitcast.249, f32[256]{0:T(256)S(1)} %bitcast.240, f32[2304]{0:T(1024)S(1)} %get-tuple-element.374, f32[256]{0:T(256)S(1)} %bitcast.257, f32[256]{0:T(256)S(1)} %bitcast.243, f32[2304]{0:T(1024)S(1)} %get-tuple-element.373, ...), kind=kOutput, calls=%fused_computation.84.clone.1 | convolution fusion | flops 28901376 | bytes 2429956 | tf_op jit(solution)/shard_map/while/body/eval_jaxpr/dot_general | solution.py:71
  108.3 2.4 %collective-permute-done.7 = f32[2,9,256]{2,1,0:T(8,128)S(1)} collective-permute-done((f32[2,9,256]{2,1,0:T(8,128)S(1)}, f32[2,9,256]{2,1,0:T(8,128)S(1)}, u32[]{:S(2)}, u32[]{:S(2)}) %collective-permute-start.7) | collective-permute-done | bytes 18464 | tf_op jit(solution)/shard_map/ppermute | solution.py:22
  114.5 3.3 %collective-permute-start.8 = (f32[16,9,256]{2,0,1:T(8,128)S(1)}, f32[16,9,256]{2,0,1:T(8,128)S(1)}, u32[]{:S(2)}, u32[]{:S(2)}) collective-permute-start(f32[16,9,256]{2,0,1:T(8,128)S(1)} %get-tuple-element.244), channel_id=1, source_target_pairs={{8,0},{12,4},{16,8},{20,12},{24,16},{28,20},{0,24},{4,28},{9,1},{1... | collective-permute-start | bytes 442376 | tf_op jit(solution)/shard_map/ppermute | solution.py:16
  124.3 31.2 %all-reduce.2.cloned.1.call-done = f32[16,9,256]{2,0,1:T(8,128)} async-done(((f32[16,9,256]{2,0,1:T(8,128)}), f32[16,9,256]{2,0,1:T(8,128)}) %all-reduce.2.cloned.1.call-update) | async-done | bytes 147472 | tf_op jit(solution)/shard_map/psum | solution.py:225
  (117 shorter events, 45.2 us)
Async XLA Ops:
  7.2 148.3 %all-reduce.2.cloned.1.call-start = ((), (), s32[]{:S(2)}) async-start(), calls=%async_computation | async-start | bytes 294912 | tf_op jit(solution)/shard_map/psum | solution.py:225
  8.2 12.3 %collective-permute-start = (f32[16,9,256]{2,1,0:T(8,128)S(1)}, f32[16,9,256]{2,1,0:T(8,128)S(1)}, u32[]{:S(2)}, u32[]{:S(2)}) collective-permute-start(f32[16,9,256]{2,1,0:T(8,128)S(1)} %copy.22), channel_id=1, source_target_pairs={{24,0},{28,4},{0,8},{4,12},{8,16},{12,20},{16,24},{20,28},{25,1},{... | collective-permute-start | bytes 442376 | tf_op jit(solution)/shard_map/ppermute | solution.py:16
  11.3 16.0 %collective-permute-start.1 = (f32[16,9,256]{2,1,0:T(8,128)S(1)}, f32[16,9,256]{2,1,0:T(8,128)S(1)}, u32[]{:S(2)}, u32[]{:S(2)}) collective-permute-start(f32[16,9,256]{2,1,0:T(8,128)S(1)} %copy.22), channel_id=1, source_target_pairs={{28,0},{0,4},{4,8},{8,12},{12,16},{16,20},{20,24},{24,28},{29,1},{... | collective-permute-start | bytes 442376 | tf_op jit(solution)/shard_map/ppermute | solution.py:16
  12.8 15.5 %collective-permute-start.2 = (f32[16,9,256]{2,1,0:T(8,128)S(1)}, f32[16,9,256]{2,1,0:T(8,128)S(1)}, u32[]{:S(2)}, u32[]{:S(2)}) collective-permute-start(f32[16,9,256]{2,1,0:T(8,128)S(1)} %copy.22), channel_id=1, source_target_pairs={{4,0},{8,4},{12,8},{16,12},{20,16},{24,20},{28,24},{0,28},{5,1},{9... | collective-permute-start | bytes 442376 | tf_op jit(solution)/shard_map/ppermute | solution.py:16
  16.0 14.8 %collective-permute-start.3 = (f32[16,9,256]{2,1,0:T(8,128)S(1)}, f32[16,9,256]{2,1,0:T(8,128)S(1)}, u32[]{:S(2)}, u32[]{:S(2)}) collective-permute-start(f32[16,9,256]{2,1,0:T(8,128)S(1)} %copy.22), channel_id=1, source_target_pairs={{8,0},{12,4},{16,8},{20,12},{24,16},{28,20},{0,24},{4,28},{9,1},{1... | collective-permute-start | bytes 442376 | tf_op jit(solution)/shard_map/ppermute | solution.py:16
  31.5 4.1 %collective-permute-start.4 = (f32[3,9,256]{2,1,0:T(8,128)S(1)}, f32[3,9,256]{2,1,0:T(8,128)S(1)}, u32[]{:S(2)}, u32[]{:S(2)}) collective-permute-start(f32[3,9,256]{2,1,0:T(8,128)S(1)} %broadcast_select_fusion.4), channel_id=1, source_target_pairs={{0,4},{4,0},{8,12},{12,8},{16,20},{20,16},{24,28},{28,24},{1,5},{5... | collective-permute-start | bytes 82952 | tf_op jit(solution)/shard_map/ppermute | solution.py:22
  36.3 26.3 %copy-start = (f32[1,1,3,2304]{3,1,2,0:T(1,128)S(1)}, f32[1,1,3,2304]{3,1,2,0:T(1,128)}, u32[]{:S(2)}) copy-start(f32[1,1,3,2304]{3,1,2,0:T(1,128)} %param.15) | copy-start | bytes 82948
  57.2 4.4 %collective-permute-start.5 = (f32[2,4,2304]{2,1,0:T(4,128)S(1)}, f32[2,4,2304]{2,1,0:T(4,128)S(1)}, u32[]{:S(2)}, u32[]{:S(2)}) collective-permute-start(f32[2,4,2304]{2,1,0:T(4,128)S(1)} %get-tuple-element.120), channel_id=1, source_target_pairs={{0,4},{4,0},{8,12},{12,8},{16,20},{20,16},{24,28},{28,24},{1,5},{5... | collective-permute-start | bytes 221192 | tf_op jit(solution)/shard_map/ppermute | solution.py:22
  62.9 4.8 %collective-permute-start.6 = (f32[3,4,2304]{2,1,0:T(4,128)S(1)}, f32[3,4,2304]{2,1,0:T(4,128)S(1)}, u32[]{:S(2)}, u32[]{:S(2)}) collective-permute-start(f32[3,4,2304]{2,1,0:T(4,128)S(1)} %pad_maximum_fusion.2), channel_id=1, source_target_pairs={{0,4},{4,0},{8,12},{12,8},{16,20},{20,16},{24,28},{28,24},{1,5},{5... | collective-permute-start | bytes 331784 | tf_op jit(solution)/shard_map/ppermute | solution.py:22
  75.0 2.2 %copy-start.1 = (f32[256,2304]{0,1:T(8,128)S(1)}, f32[256,2304]{0,1:T(8,128)}, u32[]{:S(2)}) copy-start(f32[256,2304]{0,1:T(8,128)} %fusion.182) | copy-start | bytes 7077892 | tf_op jit(solution)/shard_map/while
  83.7 1.7 %copy-start.2 = (f32[256,2304]{0,1:T(8,128)S(1)}, f32[256,2304]{0,1:T(8,128)}, u32[]{:S(2)}) copy-start(f32[256,2304]{0,1:T(8,128)} %fusion.182) | copy-start | bytes 7077892 | tf_op jit(solution)/shard_map/while
  94.0 2.2 %copy-start.1 = (f32[256,2304]{0,1:T(8,128)S(1)}, f32[256,2304]{0,1:T(8,128)}, u32[]{:S(2)}) copy-start(f32[256,2304]{0,1:T(8,128)} %fusion.182) | copy-start | bytes 7077892 | tf_op jit(solution)/shard_map/while
  102.7 1.7 %copy-start.2 = (f32[256,2304]{0,1:T(8,128)S(1)}, f32[256,2304]{0,1:T(8,128)}, u32[]{:S(2)}) copy-start(f32[256,2304]{0,1:T(8,128)} %fusion.182) | copy-start | bytes 7077892 | tf_op jit(solution)/shard_map/while
  106.7 4.0 %collective-permute-start.7 = (f32[2,9,256]{2,1,0:T(8,128)S(1)}, f32[2,9,256]{2,1,0:T(8,128)S(1)}, u32[]{:S(2)}, u32[]{:S(2)}) collective-permute-start(f32[2,9,256]{2,1,0:T(8,128)S(1)} %get-tuple-element.121), channel_id=1, source_target_pairs={{0,4},{4,0},{8,12},{12,8},{16,20},{20,16},{24,28},{28,24},{1,5},{5... | collective-permute-start | bytes 55304 | tf_op jit(solution)/shard_map/ppermute | solution.py:22
  112.0 7.9 %collective-permute-start.10 = (f32[16,9,256]{2,0,1:T(8,128)S(1)}, f32[16,9,256]{2,0,1:T(8,128)S(1)}, u32[]{:S(2)}, u32[]{:S(2)}) collective-permute-start(f32[16,9,256]{2,0,1:T(8,128)S(1)} %get-tuple-element.246), channel_id=1, source_target_pairs={{28,0},{0,4},{4,8},{8,12},{12,16},{16,20},{20,24},{24,28},{29,1},{... | collective-permute-start | bytes 442376 | tf_op jit(solution)/shard_map/ppermute | solution.py:16
  113.9 7.1 %collective-permute-start.11 = (f32[16,9,256]{2,0,1:T(8,128)S(1)}, f32[16,9,256]{2,0,1:T(8,128)S(1)}, u32[]{:S(2)}, u32[]{:S(2)}) collective-permute-start(f32[16,9,256]{2,0,1:T(8,128)S(1)} %get-tuple-element.245), channel_id=1, source_target_pairs={{24,0},{28,4},{0,8},{4,12},{8,16},{12,20},{16,24},{20,28},{25,1},{... | collective-permute-start | bytes 442376 | tf_op jit(solution)/shard_map/ppermute | solution.py:16
  114.5 6.8 %collective-permute-start.8 = (f32[16,9,256]{2,0,1:T(8,128)S(1)}, f32[16,9,256]{2,0,1:T(8,128)S(1)}, u32[]{:S(2)}, u32[]{:S(2)}) collective-permute-start(f32[16,9,256]{2,0,1:T(8,128)S(1)} %get-tuple-element.244), channel_id=1, source_target_pairs={{8,0},{12,4},{16,8},{20,12},{24,16},{28,20},{0,24},{4,28},{9,1},{1... | collective-permute-start | bytes 442376 | tf_op jit(solution)/shard_map/ppermute | solution.py:16
  117.8 5.1 %collective-permute-start.9 = (f32[16,9,256]{2,0,1:T(8,128)S(1)}, f32[16,9,256]{2,0,1:T(8,128)S(1)}, u32[]{:S(2)}, u32[]{:S(2)}) collective-permute-start(f32[16,9,256]{2,0,1:T(8,128)S(1)} %get-tuple-element.247), channel_id=1, source_target_pairs={{4,0},{8,4},{12,8},{16,12},{20,16},{24,20},{28,24},{0,28},{5,1},{9... | collective-permute-start | bytes 442376 | tf_op jit(solution)/shard_map/ppermute | solution.py:16
Sparse Core Ops, SparseCore 0:
  123.8 31.6 all-reduce.1
where the time goes:
time: 164 us
  waiting for transfers between devices  55.2 us (34%)
  matrix products  43.7 us (27%)
  starting transfers between devices  21.6 us (13%)
  other arithmetic  17.5 us (11%)
  between operations  15.6 us (10%)
  local copies, waits for them, and re-layouts  9.71 us (6%)
    psum x1, waiting for transfers between devices, shards(): gauss_grad = lax.psum(block_grads, 'view')  31.2 us
    ppermute x8, starting transfers between devices, shifted(): return lax.ppermute(block, axis, route)  15.3 us
    ppermute x8, waiting for transfers between devices, shifted(): return lax.ppermute(block, axis, route)  13 us
    ppermute x4, waiting for transfers between devices, partner(): return lax.ppermute(value, axis, pairs)  10.9 us
    dot_general x2, matrix products, backward_task(): jnp.dot(lower_tri, log_trans, precision=precise, preferred_element_type=j...  9.84 us
    dot_general x2, matrix products, forward_task(): jnp.dot(lower_tri, log_trans, precision=precise, preferred_element_type=j...  9.51 us
    dot_general x2, matrix products, backward_task(): jnp.dot(upper_tri, weights * shaded, precision=precise, preferred_element...  9.07 us
    ppermute x4, starting transfers between devices, partner(): return lax.ppermute(value, axis, pairs)  6.28 us
  transfers between devices with their start and end apart: 13, of which 12 were waited for; matrix products, arithmetic and copies ran while one was open for 3% of the time, Pallas kernels for 0%

commit v1 on v0

v1 whole, which is shorter than its diff:
```python
import functools

import jax
import jax.numpy as jnp
from jax import lax
from jax.experimental import pallas as pl
from jax.experimental.pallas import tpu as pltpu
from jax.sharding import PartitionSpec as P

TILE = 48
LANES = 128
LOG2E = 1.4426950408889634
MESH = pl.DeviceIdType.MESH
F32 = jnp.float32
BF16 = jnp.bfloat16


def split(value):
    high = value.astype(BF16)
    return high, (value - high.astype(F32)).astype(BF16)


def dot(left, right):
    return jnp.dot(left, right, preferred_element_type=F32)


def dot_nt(left, right):
    return lax.dot_general(left, right, (((1,), (1,)), ((), ())), preferred_element_type=F32)


def cell_peers(cells, me):
    side = me % 2
    base = me - side
    peers = [((base + 1 - side) % cells, 0, 3 - side, 2 + side)]
    for pair in (-1, 1):
        for other in (0, 1):
            cell = (base + 2 * pair + other + cells) % cells
            peers.append((cell, pair, 2 * pair + 2 + other, side + 2 - 2 * pair))
    return peers


def pair_ids(even, odd, slots):
    count = even[0:1, 0:1]
    ids = []
    for s in range(slots + 1):
        picked = even[0:1, 1 + min(s, slots - 1) : 2 + min(s, slots - 1)]
        for k in range(slots):
            picked = jnp.where(count == s - k, odd[0:1, 1 + k : 2 + k], picked)
        ids.append(picked)
    return ids


def fetch_kernel(
    cells, slots, info_ref, gauss_ref, tgt_ref, infos, blocks, tgts, resp, got,
    info_send, info_recv, tgt_send, tgt_recv, blk_send, blk_recv,
):
    me = lax.axis_index("cell")
    side = me % 2
    per_block = gauss_ref.shape[0]
    peers = cell_peers(cells, me)
    barrier = pltpu.get_barrier_semaphore()
    for cell, _, _, _ in peers:
        pl.semaphore_signal(barrier, inc=1, device_id={"cell": cell}, device_id_type=MESH)
    pl.semaphore_wait(barrier, len(peers))
    infos[2 + side] = info_ref[...]
    sends = []
    for n, (cell, _, _, theirs) in enumerate(peers):
        copy = pltpu.make_async_remote_copy(
            info_ref, infos.at[theirs], info_send.at[n], info_recv.at[theirs],
            device_id={"cell": cell}, device_id_type=MESH,
        )
        copy.start()
        sends.append(copy)
    partner = peers[0][0]
    tgt_copy = pltpu.make_async_remote_copy(
        tgt_ref.at[1 - side], tgts.at[side], tgt_send, tgt_recv,
        device_id={"cell": partner}, device_id_type=MESH,
    )
    tgt_copy.start()
    tgts[side] = tgt_ref[side]
    for n, (cell, _, mine, _) in enumerate(peers):
        pltpu.make_async_remote_copy(
            info_ref, infos.at[mine], info_send.at[n], info_recv.at[mine],
            device_id={"cell": cell}, device_id_type=MESH,
        ).wait_recv()
    for pair in (-1, 1, 0):
        ids = pair_ids(infos[2 * pair + 2], infos[2 * pair + 3], slots)
        for s in range(slots + 1):
            local = ids[s] - me * per_block
            total = jnp.zeros(gauss_ref.shape[1:], F32)
            for b in range(per_block):
                total = jnp.where(local == b, gauss_ref[b], total)
            resp[pair + 1, s] = total
        for n, (cell, distance, _, theirs) in enumerate(peers):
            if distance == pair:
                copy = pltpu.make_async_remote_copy(
                    resp.at[pair + 1], got.at[theirs], blk_send.at[n], blk_recv.at[theirs],
                    device_id={"cell": cell}, device_id_type=MESH,
                )
                copy.start()
                sends.append(copy)
    total = resp[1]
    for n, (cell, distance, mine, _) in enumerate(peers):
        pltpu.make_async_remote_copy(
            resp.at[distance + 1], got.at[mine], blk_send.at[n], blk_recv.at[mine],
            device_id={"cell": cell}, device_id_type=MESH,
        ).wait_recv()
        total = total + got[mine]
    blocks[...] = total
    tgt_copy.wait_recv()
    tgt_copy.wait_send()
    for copy in sends:
        copy.wait_send()


def fetch(cells, slots, info, gaussians, halves):
    pack = (slots + 1,) + gaussians.shape[1:]
    vmem = pl.BlockSpec(memory_space=pltpu.VMEM)
    dma = pltpu.SemaphoreType.DMA
    return pl.pallas_call(
        functools.partial(fetch_kernel, cells, slots),
        out_shape=(
            jax.ShapeDtypeStruct((6,) + info.shape, jnp.int32),
            jax.ShapeDtypeStruct(pack, F32),
            jax.ShapeDtypeStruct(halves.shape, F32),
        ),
        in_specs=[vmem] * 3,
        out_specs=(vmem,) * 3,
        scratch_shapes=[
            pltpu.VMEM((3,) + pack, F32),
            pltpu.VMEM((6,) + pack, F32),
            dma((5,)), dma((6,)), dma, dma, dma((5,)), dma((6,)),
        ],
        compiler_params=pltpu.CompilerParams(
            collective_id=0, has_side_effects=True, vmem_limit_bytes=24 * 2**20
        ),
        name="fetch_blocks",
    )(info, gaussians, halves)


def render_kernel(
    slots, chunk, par_ref, infos, shift_ref, tgt_ref, grad_ref, img_ref, alphas, weights, w_hi, w_lo, moments, cgrads
):
    side = lax.axis_index("cell") % 2
    half = tgt_ref.shape[2]
    size = par_ref.shape[2]
    segs = slots + 1
    even, odd = infos[2], infos[3]
    count, ray_even, ray_odd = even[0:1, 0:1], even[0:1, slots + 1 : slots + 2], odd[0:1, slots + 1 : slots + 2]
    shift_x, shift_y = shift_ref[0:1, 0:1], shift_ref[0:1, 1:2]
    centre = (TILE - 1) / 2.0
    row_ids = lax.broadcasted_iota(jnp.int32, (size, size), 0)
    col_ids = lax.broadcasted_iota(jnp.int32, (size, size), 1)
    before = (row_ids < col_ids).astype(F32).astype(BF16)
    after = (row_ids > col_ids).astype(F32).astype(BF16)
    zero3 = jnp.zeros((5, size), F32)
    moments[...] = jnp.zeros_like(moments)
    cgrads[...] = jnp.zeros_like(cgrads)

    def place(ids):
        ids = ids.astype(F32)
        row = jnp.floor((ids + 0.5) * (1.0 / TILE))
        return ids - TILE * row - centre, row - centre

    def colour_rows(s):
        colours = jnp.concatenate([par_ref[s, 6:9], zero3], axis=0)
        in_even = (count > s).astype(F32)
        both = jnp.concatenate([colours * in_even, colours * (1.0 - in_even)], axis=0)
        high = both.astype(BF16).astype(F32)
        return high, both - high

    @pl.loop(0, half // chunk)
    def _(step):
        start = pl.multiple_of(step * chunk, chunk)
        first = side * half + start
        x_0, y_0 = place(first + lax.broadcasted_iota(jnp.int32, (chunk, size), 0))
        x_0 = x_0 - shift_x
        y_0 = y_0 - shift_y
        lane_ids = first + lax.broadcasted_iota(jnp.int32, (16, chunk), 1)
        carry = jnp.zeros((chunk, 1), F32)
        image = jnp.zeros((32, chunk), F32)
        for s in range(segs):
            row = lambda r: par_ref[s, r : r + 1]
            dx = x_0 - row(0)
            dy = y_0 - row(1)
            power = dx * ((-0.5 * LOG2E) * row(2) * dx + (-LOG2E) * row(3) * dy) + ((-0.5 * LOG2E) * row(4) * dy) * dy
            alpha = row(5) * jnp.exp2(power)
            ell = jnp.log(1.0 - alpha)
            high, low = split(ell)
            prefix = dot(high, before) + dot(low, before) + carry
            weight = alpha * jnp.exp(prefix)
            carry = jnp.where(count == s + 1, 0.0, prefix[:, size - 1 :] + ell[:, size - 1 :])
            high, low = split(weight)
            alphas[s] = alpha
            weights[s] = weight
            w_hi[s] = high
            w_lo[s] = low
            c_hi, c_lo = colour_rows(s)
            colours = jnp.concatenate([c_hi, c_lo], axis=0).astype(BF16)
            image = image + dot_nt(colours, high) + dot_nt(colours, low)
        in_tile = lax.broadcasted_iota(jnp.int32, (16, chunk), 0) < 8
        live = (lane_ids < jnp.where(in_tile, ray_even, ray_odd)).astype(F32)
        rendered = (image[:16] + image[16:]) * live
        cols = pl.ds(start, chunk)
        img_ref[0, :, cols] = rendered[:8]
        img_ref[1, :, cols] = rendered[8:]
        target = jnp.concatenate([tgt_ref[0, :, cols], tgt_ref[1, :, cols]], axis=0)
        residual = (rendered - target) * live
        r_hi = residual.astype(BF16).astype(F32)
        r_lo = residual - r_hi
        spread = jnp.concatenate([r_hi, r_lo, r_hi, jnp.zeros((LANES - 48, chunk), F32)], axis=0)
        spread = jnp.transpose(spread).astype(BF16)
        r_rows = jnp.concatenate([r_hi, r_lo], axis=0).astype(BF16)
        x_l, y_l = place(lane_ids[:1])
        squares = [x_l * x_l, x_l * y_l, y_l * y_l]
        sq_hi = [q.astype(BF16).astype(F32) for q in squares]
        none = jnp.zeros_like(x_l)
        features = [none + 1.0, x_l, y_l] + sq_hi + [none] * 5 + [q - h for q, h in zip(squares, sq_hi)] + [none] * 2
        features = jnp.concatenate(features, axis=0).astype(BF16)
        carry = jnp.zeros((chunk, 1), F32)
        for s in reversed(range(segs)):
            c_hi, c_lo = colour_rows(s)
            colours = jnp.concatenate([c_hi, c_hi, c_lo, jnp.zeros((LANES - 48, size), F32)], axis=0).astype(BF16)
            product = weights[s] * dot(spread, colours)
            high, low = split(product)
            tail = dot(high, after) + dot(low, after) + carry
            carry = jnp.where(count == s, 0.0, tail[:, :1] + product[:, :1])
            alpha = alphas[s]
            rest = 1.0 - alpha
            inverse = pl.reciprocal(rest, approx=True)
            inverse = inverse * (2.0 - rest * inverse)
            high, low = split(product - alpha * inverse * tail)
            moments[s] += dot(features, high) + dot(features, low)
            cgrads[s] += dot(r_rows, w_hi[s]) + dot(r_rows, w_lo[s])

    for s in range(segs):
        row = lambda r: par_ref[s, r : r + 1]
        mean_x, mean_y = row(0) + shift_x, row(1) + shift_y
        m = [moments[s, k : k + 1] for k in range(3)] + [
            moments[s, k : k + 1] + moments[s, k + 8 : k + 9] for k in range(3, 6)
        ]
        along_x = m[1] - mean_x * m[0]
        along_y = m[2] - mean_y * m[0]
        square_x = m[3] - 2.0 * mean_x * m[1] + mean_x * mean_x * m[0]
        cross_xy = m[4] - mean_x * m[2] - mean_y * m[1] + mean_x * mean_y * m[0]
        square_y = m[5] - 2.0 * mean_y * m[2] + mean_y * mean_y * m[0]
        cg = cgrads[s, :16] + cgrads[s, 16:]
        grad_ref[s, 0:1] = row(2) * along_x + row(3) * along_y
        grad_ref[s, 1:2] = row(3) * along_x + row(4) * along_y
        grad_ref[s, 2:3] = -0.5 * square_x
        grad_ref[s, 3:4] = -cross_xy
        grad_ref[s, 4:5] = -0.5 * square_y
        grad_ref[s, 5:6] = m[0] / row(5)
        grad_ref[s, 6:9] = jnp.where(count > s, cg[0:3], cg[8:11])


def render(slots, params, infos, shift, halves):
    segs, _, size = params.shape
    half = halves.shape[2]
    chunk = next(c for c in (384, 256, 128) if half % c == 0)
    vmem = pl.BlockSpec(memory_space=pltpu.VMEM)
    return pl.pallas_call(
        functools.partial(render_kernel, slots, chunk),
        out_shape=(
            jax.ShapeDtypeStruct(params.shape, F32),
            jax.ShapeDtypeStruct(halves.shape, F32),
        ),
        in_specs=[vmem] * 4,
        out_specs=(vmem,) * 2,
        scratch_shapes=[
            pltpu.VMEM((segs, chunk, size), F32),
            pltpu.VMEM((segs, chunk, size), F32),
            pltpu.VMEM((segs, chunk, size), BF16),
            pltpu.VMEM((segs, chunk, size), BF16),
            pltpu.VMEM((segs, 16, size), F32),
            pltpu.VMEM((segs, 32, size), F32),
        ],
        compiler_params=pltpu.CompilerParams(vmem_limit_bytes=40 * 2**20),
        name="render_pair",
    )(params, infos, shift, halves)


def reduce_kernel(
    cells, views, slots, grad_ref, infos, img_ref, out_ref, imgs, got, part, quarter,
    img_send, img_recv, seg_send, seg_recv, part_send, part_recv, full_send, full_recv,
):
    me = lax.axis_index("cell")
    view = lax.axis_index("view")
    side = me % 2
    per_block = out_ref.shape[0]
    share = per_block // views
    peers = cell_peers(cells, me)
    others = [(view + k) % views for k in range(1, views)]
    barrier = pltpu.get_barrier_semaphore()
    for cell, _, _, _ in peers:
        pl.semaphore_signal(barrier, inc=1, device_id={"cell": cell}, device_id_type=MESH)
    for other in others:
        pl.semaphore_signal(barrier, inc=1, device_id={"view": other}, device_id_type=MESH)
    pl.semaphore_wait(barrier, len(peers) + len(others))
    sends = []
    for n, (cell, _, _, theirs) in enumerate(peers):
        copy = pltpu.make_async_remote_copy(
            grad_ref, got.at[theirs], seg_send.at[n], seg_recv.at[theirs],
            device_id={"cell": cell}, device_id_type=MESH,
        )
        copy.start()
        sends.append(copy)
    img_copy = pltpu.make_async_remote_copy(
        img_ref.at[1 - side], imgs.at[side], img_send, img_recv,
        device_id={"cell": peers[0][0]}, device_id_type=MESH,
    )
    img_copy.start()
    imgs[side] = img_ref[side]
    for n, (cell, _, mine, _) in enumerate(peers):
        pltpu.make_async_remote_copy(
            grad_ref, got.at[mine], seg_send.at[n], seg_recv.at[mine],
            device_id={"cell": cell}, device_id_type=MESH,
        ).wait_recv()
    got[2 + side] = grad_ref[...]
    locals_, sums = [], []
    for pair in (-1, 0, 1):
        ids = pair_ids(infos[2 * pair + 2], infos[2 * pair + 3], slots)
        for s in range(slots + 1):
            locals_.append(ids[s] - me * per_block)
            sums.append((pair, s))
    for b in range(per_block):
        total = jnp.zeros(out_ref.shape[1:], F32)
        for local, (pair, s) in zip(locals_, sums):
            total = total + jnp.where(local == b, got[2 * pair + 2, s] + got[2 * pair + 3, s], 0.0)
        part[b // share, b % share] = total
    for k, other in enumerate(others):
        copy = pltpu.make_async_remote_copy(
            part.at[other], quarter.at[k], part_send.at[k], part_recv.at[k],
            device_id={"view": other}, device_id_type=MESH,
        )
        copy.start()
        sends.append(copy)
    total = part[view]
    for k in range(views - 1):
        sends[len(peers) + k].wait_recv()
        total = total + quarter[k]
    mine = pl.ds(view * share, share)
    out_ref[mine] = total
    for k, other in enumerate(others):
        copy = pltpu.make_async_remote_copy(
            out_ref.at[mine], out_ref.at[mine], full_send.at[k], full_recv.at[k],
            device_id={"view": other}, device_id_type=MESH,
        )
        copy.start()
        sends.append(copy)
    for k in range(views - 1):
        theirs = pl.ds(((view + views - 1 - k) % views) * share, share)
        pltpu.make_async_remote_copy(
            out_ref.at[theirs], out_ref.at[theirs], full_send.at[k], full_recv.at[k],
            device_id={"view": others[k]}, device_id_type=MESH,
        ).wait_recv()
    img_copy.wait_recv()
    img_copy.wait_send()
    for copy in sends:
        copy.wait_send()


def reduce_grads(cells, views, slots, shape, grads, infos, images):
    vmem = pl.BlockSpec(memory_space=pltpu.VMEM)
    dma = pltpu.SemaphoreType.DMA
    share = shape[0] // views
    return pl.pallas_call(
        functools.partial(reduce_kernel, cells, views, slots),
        out_shape=(
            jax.ShapeDtypeStruct(shape, F32),
            jax.ShapeDtypeStruct(images.shape, F32),
        ),
        in_specs=[vmem] * 3,
        out_specs=(vmem,) * 2,
        scratch_shapes=[
            pltpu.VMEM((6,) + grads.shape, F32),
            pltpu.VMEM((views, share) + shape[1:], F32),
            pltpu.VMEM((views - 1, share) + shape[1:], F32),
            dma, dma, dma((5,)), dma((6,)),
            dma((views - 1,)), dma((views - 1,)), dma((views - 1,)), dma((views - 1,)),
        ],
        compiler_params=pltpu.CompilerParams(
            collective_id=1, has_side_effects=True, vmem_limit_bytes=24 * 2**20
        ),
        name="reduce_grads",
    )(grads, infos, images)


def shards(cells, views, gaussians, seg_count, seg_block, ray_count, camera_shift, target):
    slots = seg_block.shape[2]
    pixels = target.shape[3]
    fields = jnp.concatenate([seg_count[0], seg_block[0, 0], ray_count[0]])
    info = jnp.broadcast_to(jnp.pad(fields, (0, LANES - fields.shape[0]))[None], (8, LANES))
    halves = target[0, 0].reshape(3, 2, pixels // 2).transpose(1, 0, 2)
    halves = jnp.pad(halves, ((0, 0), (0, 5), (0, 0)))
    infos, params, targets = fetch(cells, slots, info, gaussians, halves)
    grads, images = render(slots, params, infos, camera_shift, targets)
    gauss_grad, images = reduce_grads(cells, views, slots, gaussians.shape, grads, infos, images)
    image = images[:, :3].transpose(1, 0, 2).reshape(3, pixels)
    return (image[None, None], gauss_grad)


def solution(mesh):
    placed = (
        P("cell", None, None),
        P("view", "cell"),
        P("view", "cell", None),
        P("view", "cell"),
        P("view", None),
        P("view", "cell", None, None),
    )
    return jax.shard_map(
        functools.partial(shards, mesh.shape["cell"], mesh.shape["view"]),
        mesh=mesh,
        in_specs=placed,
        out_specs=(P("view", "cell", None, None), P("cell", None, None)),
        check_vma=False,
    )
```

time: 164 us -> 53 us (0.32)
  waiting for transfers between devices: 55.2 us -> 0 us
  Pallas kernels: 0 us -> 46.6 us
  matrix products: 43.7 us -> 0 us
  starting transfers between devices: 21.6 us -> 0 us
  other arithmetic: 17.5 us -> 1.55 us
  between operations: 15.6 us -> 2.03 us
  local copies, waits for them, and re-layouts: 9.71 us -> 2.16 us
    pallas_call x0 -> x3, Pallas kernels: none -> 46.6 us  [the longest x1 17.4 us: fetch(): pl.pallas_call(functools.partial(fetch_kernel, cells, slots), out_shape=(...]
    dot_general x15 -> x0, matrix products: 43.7 us -> none  [the longest x2 9.84 us: backward_task(): jnp.dot(lower_tri, log_trans, precision=precise, preferred_element_type=j...]
    psum x1 -> x0, waiting for transfers between devices: 31.2 us -> none  [shards(): gauss_grad = lax.psum(block_grads, 'view')]
    ppermute x12 -> x0, waiting for transfers between devices: 24 us -> none  [the longest x8 13 us: shifted(): return lax.ppermute(block, axis, route)]
    ppermute x12 -> x0, starting transfers between devices: 21.6 us -> none  [the longest x8 15.3 us: shifted(): return lax.ppermute(block, axis, route)]
    sub x4 -> x0, other arithmetic: 4.93 us -> none  [pixel_frame(): pix_y = (pixel_ids // TILE).astype(jnp.float32) - centre - shift[1]]
    mul x10 -> x0, other arithmetic: 4.83 us -> none  [the longest x2 2.55 us: gradient_rows(): pix_y * pix_y]
    reduce_sum x3 -> x0, other arithmetic: 4.64 us -> none  [the longest x2 4.59 us: forward_task(): totals = jnp.sum(log_trans, axis=0)]
  transfers between devices with their start and end apart: 13 -> 0, of which waited for: 12 -> 0; matrix products, arithmetic and copies ran while one was open for 3% -> 0% of each run, Pallas kernels for 0% -> 0%
where the time goes in v1:
time: 53 us; the launch traced here: 52.4 us
  Pallas kernels  46.6 us (88%)
  local copies, waits for them, and re-layouts  2.16 us (4%)
  between operations  2.03 us (4%)
  other arithmetic  1.55 us (3%)
    pallas_call x1, Pallas kernels, fetch(): pl.pallas_call(functools.partial(fetch_kernel, cells, slots), out_shape=(...  17.4 us
    pallas_call x1, Pallas kernels, reduce_grads(): pl.pallas_call(functools.partial(reduce_kernel, cells, views, slots), out...  16.6 us
    pallas_call x1, Pallas kernels, render(): pl.pallas_call(functools.partial(render_kernel, slots, chunk), out_shape=...  12.7 us
    unnamed x7, local copies, waits for them, and re-layouts  2.13 us

profile of v1, /device:TPU:0, one launch (start us, length us, event | category | flops | bytes accessed | tf_op | source)
XLA Modules:
  0.0 52.4 jit_solution(2960169511465345042)
XLA Ops:
  0.6 0.0 copy-start.1
  2.0 0.7 %pad_add_fusion = s32[5]{0:T(128)S(1)} fusion(s32[1]{0:T(128)} %bitcast.10, s32[3]{0:T(128)} %bitcast.13, s32[1]{0:T(128)} %bitcast.9), kind=kLoop, calls=%fused_computation | loop fusion | flops 10 | bytes 40 | tf_op jit(solution)/shard_map/concatenate | solution.py:392
  2.7 0.8 %reduce = f32[3,2304]{1,0:T(4,128)S(1)} reduce(f32[1,1,3,2304]{3,1,2,0:T(1,128)} %param.11, f32[]{:T(128)} %constant.13), dimensions={0,1}, to_apply=%param.11.reduce_sub_computation | reduce | bytes 55300 | tf_op args[5]
  3.6 0.0 copy-done.1
  3.6 0.1 copy.11.gauss_ref
  3.7 17.4 %fetch_blocks.1 = (s32[6,8,128]{2,1,0:T(8,128)S(1)}, f32[4,9,256]{2,1,0:T(8,128)S(1)}, f32[2,8,1152]{2,1,0:T(8,128)S(1)}) custom-call(s32[8,128]{1,0:T(8,128)S(1)} %broadcast_in_dim.2.info_ref, f32[16,9,256]{2,1,0:T(8,128)S(1)} %copy.11.gauss_ref, f32[2,8,1152]{2,1,0:T(8,128)S(1)} %pad.9.tgt_ref), custom_call_target="tpu_custom_call" | custom-call | tf_op jit(solution)/shard_map/fetch_blocks/pallas_call | solution.py:120
  21.0 0.0 copy-start
  21.1 0.6 %copy-done = f32[1,2]{1,0:T(1,128)S(1)} copy-done((f32[1,2]{1,0:T(1,128)S(1)}, f32[1,2]{1,0:T(1,128)}, u32[]{:S(2)}) %copy-start) | copy-done | bytes 32
  21.7 12.7 %render_pair.1 = (f32[4,9,256]{2,1,0:T(8,128)S(1)}, f32[2,8,1152]{2,1,0:T(8,128)S(1)}) custom-call(f32[4,9,256]{2,1,0:T(8,128)S(1)} %get-tuple-element.9.par_ref, s32[6,8,128]{2,1,0:T(8,128)S(1)} %get-tuple-element.10.infos, f32[1,2]{1,0:T(1,128)S(1)} %copy-done, f32[2,8,1152]{2,1,0:T(8,128)S(1)} %get-tuple-element.11.tgt_ref), custom_call_target="tpu_custom_call" | custom-call | tf_op jit(solution)/shard_map/render_pair/pallas_call | solution.py:262
  34.4 16.6 %reduce_grads.1 = (f32[16,9,256]{2,1,0:T(8,128)S(1)}, f32[2,8,1152]{2,1,0:T(8,128)S(1)}) custom-call(f32[4,9,256]{2,1,0:T(8,128)S(1)} %get-tuple-element.12.grad_ref, s32[6,8,128]{2,1,0:T(8,128)S(1)} %get-tuple-element.10.infos, f32[2,8,1152]{2,1,0:T(8,128)S(1)} %get-tuple-element.13.img_ref), custom_call_target="tpu_custom_call" | custom-call | tf_op jit(solution)/shard_map/reduce_grads/pallas_call | solution.py:367
  51.0 0.6 %copy.12 = f32[1,1,3,2304]{3,1,2,0:T(1,128)} copy(f32[1,1,3,2304]{3,2,1,0:T(4,128)S(1)} %bitcast.12) | data formatting | bytes 55296
  51.6 0.8 %copy.13 = f32[16,9,256]{2,0,1:T(8,128)} copy(f32[16,9,256]{2,1,0:T(8,128)S(1)} %get-tuple-element.19) | data formatting | bytes 294912
  (4 shorter events, 0.0 us)
Async XLA Ops:
  0.6 2.9 %copy-start.1 = (f32[16,9,256]{2,0,1:T(8,128)S(1)}, f32[16,9,256]{2,0,1:T(8,128)}, u32[]{:S(2)}) copy-start(f32[16,9,256]{2,0,1:T(8,128)} %param.6) | copy-start | bytes 442372
  21.0 0.7 %copy-start = (f32[1,2]{1,0:T(1,128)S(1)}, f32[1,2]{1,0:T(1,128)}, u32[]{:S(2)}) copy-start(f32[1,2]{1,0:T(1,128)} %shift_ref.1) | copy-start | bytes 28

commit v2 on v1

v2 whole, which is shorter than its diff:
```python
import functools

import jax
import jax.numpy as jnp
from jax import lax
from jax.experimental import pallas as pl
from jax.experimental.pallas import tpu as pltpu
from jax.sharding import PartitionSpec as P

TILE = 48
LANES = 128
LOG2E = 1.4426950408889634
MESH = pl.DeviceIdType.MESH
F32 = jnp.float32
BF16 = jnp.bfloat16


def split(value):
    high = value.astype(BF16)
    return high, (value - high.astype(F32)).astype(BF16)


def dot(left, right):
    return jnp.dot(left, right, preferred_element_type=F32)


def dot_nt(left, right):
    return lax.dot_general(left, right, (((1,), (1,)), ((), ())), preferred_element_type=F32)


def cell_peers(cells, me):
    side = me % 2
    base = me - side
    peers = [((base + 1 - side) % cells, 0, 3 - side, 2 + side)]
    for pair in (-1, 1):
        for other in (0, 1):
            cell = (base + 2 * pair + other + cells) % cells
            peers.append((cell, pair, 2 * pair + 2 + other, side + 2 - 2 * pair))
    return peers


def pair_ids(even, odd, slots):
    count = even[0:1, 0:1]
    ids = []
    for s in range(slots + 1):
        picked = even[0:1, 1 + min(s, slots - 1) : 2 + min(s, slots - 1)]
        for k in range(slots):
            picked = jnp.where(count == s - k, odd[0:1, 1 + k : 2 + k], picked)
        ids.append(picked)
    return ids


def packed_rows(blocks, rows):
    return 2 * blocks * rows


def put(ref, blocks, index, value):
    rows, size = value.shape
    for h in range(2):
        at = (h * blocks + index) * rows
        ref[at : at + rows] = value[:, h * (size // 2) : (h + 1) * (size // 2)]


def take(value, blocks, index, rows):
    parts = []
    for h in range(2):
        at = (h * blocks + index) * rows
        parts.append(value[at : at + rows])
    return jnp.concatenate(parts, axis=1)


def fetch_kernel(
    cells, slots, count_ref, block_ref, ray_ref, gauss_ref, tgt_ref, infos, blocks, tgts, info, half_out, resp, got,
    info_send, info_recv, tgt_send, tgt_recv, blk_send, blk_recv,
):
    me = lax.axis_index("cell")
    side = me % 2
    per_block, rows, _ = gauss_ref.shape
    half = tgts.shape[2]
    peers = cell_peers(cells, me)
    barrier = pltpu.get_barrier_semaphore()
    for cell, _, _, _ in peers:
        pl.semaphore_signal(barrier, inc=1, device_id={"cell": cell}, device_id_type=MESH)
    lane = lax.broadcasted_iota(jnp.int32, info.shape, 1)
    fields = jnp.where(lane == 0, count_ref[0, 0], 0)
    for s in range(slots):
        fields = jnp.where(lane == 1 + s, block_ref[0, 0, s], fields)
    fields = jnp.where(lane == 1 + slots, ray_ref[0, 0], fields)
    info[...] = fields
    infos[2 + side] = fields
    other_half = pl.multiple_of((1 - side) * half, LANES)
    own_half = pl.multiple_of(side * half, LANES)
    blank = jnp.zeros((8 - tgt_ref.shape[2], half), F32)
    half_out[...] = jnp.concatenate([tgt_ref[0, 0, :, pl.ds(other_half, half)], blank], axis=0)
    tgts[side] = jnp.concatenate([tgt_ref[0, 0, :, pl.ds(own_half, half)], blank], axis=0)
    pl.semaphore_wait(barrier, len(peers))
    sends = []
    for n, (cell, _, _, theirs) in enumerate(peers):
        copy = pltpu.make_async_remote_copy(
            info, infos.at[theirs], info_send.at[n], info_recv.at[theirs],
            device_id={"cell": cell}, device_id_type=MESH,
        )
        copy.start()
        sends.append(copy)
    tgt_copy = pltpu.make_async_remote_copy(
        half_out, tgts.at[side], tgt_send, tgt_recv,
        device_id={"cell": peers[0][0]}, device_id_type=MESH,
    )
    tgt_copy.start()
    for pair in (-1, 1, 0):
        for n, (cell, distance, mine, _) in enumerate(peers):
            if distance == pair:
                pltpu.make_async_remote_copy(
                    info, infos.at[mine], info_send.at[n], info_recv.at[mine],
                    device_id={"cell": cell}, device_id_type=MESH,
                ).wait_recv()
        ids = pair_ids(infos[2 * pair + 2], infos[2 * pair + 3], slots)
        for s in range(slots + 1):
            local = jnp.broadcast_to(ids[s] - me * per_block, gauss_ref.shape[1:])
            total = jnp.zeros(gauss_ref.shape[1:], F32)
            for b in range(per_block):
                total = jnp.where(local == b, gauss_ref[b], total)
            put(resp.at[pair + 1], slots + 1, s, total)
        for n, (cell, distance, _, theirs) in enumerate(peers):
            if distance == pair:
                copy = pltpu.make_async_remote_copy(
                    resp.at[pair + 1], got.at[theirs], blk_send.at[n], blk_recv.at[theirs],
                    device_id={"cell": cell}, device_id_type=MESH,
                )
                copy.start()
                sends.append(copy)
    total = resp[1]
    for n, (cell, distance, mine, _) in enumerate(peers):
        pltpu.make_async_remote_copy(
            resp.at[distance + 1], got.at[mine], blk_send.at[n], blk_recv.at[mine],
            device_id={"cell": cell}, device_id_type=MESH,
        ).wait_recv()
        total = total + got[mine]
    for s in range(slots + 1):
        blocks[s] = take(total, slots + 1, s, rows)
    tgt_copy.wait_recv()
    tgt_copy.wait_send()
    for copy in sends:
        copy.wait_send()


def fetch(cells, seg_count, seg_block, ray_count, gaussians, target):
    slots = seg_block.shape[2]
    _, rows, size = gaussians.shape
    half = target.shape[3] // 2
    pack = (packed_rows(slots + 1, rows), size // 2)
    vmem = pl.BlockSpec(memory_space=pltpu.VMEM)
    smem = pl.BlockSpec(memory_space=pltpu.SMEM)
    dma = pltpu.SemaphoreType.DMA
    return pl.pallas_call(
        functools.partial(fetch_kernel, cells, slots),
        out_shape=(
            jax.ShapeDtypeStruct((6, 8, LANES), jnp.int32),
            jax.ShapeDtypeStruct((slots + 1, rows, size), F32),
            jax.ShapeDtypeStruct((2, 8, half), F32),
        ),
        in_specs=[smem] * 3 + [vmem] * 2,
        out_specs=(vmem,) * 3,
        scratch_shapes=[
            pltpu.VMEM((8, LANES), jnp.int32),
            pltpu.VMEM((8, half), F32),
            pltpu.VMEM((3,) + pack, F32),
            pltpu.VMEM((6,) + pack, F32),
            dma((5,)), dma((6,)), dma, dma, dma((5,)), dma((6,)),
        ],
        compiler_params=pltpu.CompilerParams(
            collective_id=0, has_side_effects=True, vmem_limit_bytes=24 * 2**20
        ),
        name="fetch_blocks",
    )(seg_count, seg_block, ray_count, gaussians, target)


def render_kernel(
    slots, chunk, sub, par_ref, infos, shift_ref, tgt_ref, grad_ref, img_ref,
    alphas, weights, w_pair, stage, h_pair, x_pos, y_pos, moments, cgrads,
):
    side = lax.axis_index("cell") % 2
    half = tgt_ref.shape[2]
    size = par_ref.shape[2]
    segs = slots + 1
    even, odd = infos[2], infos[3]
    count, ray_even, ray_odd = even[0:1, 0:1], even[0:1, slots + 1 : slots + 2], odd[0:1, slots + 1 : slots + 2]
    shift_x, shift_y = shift_ref[0:1, 0:1], shift_ref[0:1, 1:2]
    centre = (TILE - 1) / 2.0
    row_ids = lax.broadcasted_iota(jnp.int32, (size, size), 0)
    col_ids = lax.broadcasted_iota(jnp.int32, (size, size), 1)
    before = (row_ids < col_ids).astype(F32).astype(BF16)
    after = (row_ids > col_ids).astype(F32).astype(BF16)
    before = jnp.concatenate([before, before], axis=0)
    after = jnp.concatenate([after, after], axis=0)
    blank = jnp.zeros((5, size), F32)
    moments[...] = jnp.zeros_like(moments)
    cgrads[...] = jnp.zeros_like(cgrads)
    parts = [slice(r, r + sub) for r in range(0, chunk, sub)]

    def place(ids):
        ids = ids.astype(F32)
        row = jnp.floor((ids + 0.5) * (1.0 / TILE))
        return ids - TILE * row - centre, row - centre

    def colour_rows(s):
        colours = jnp.concatenate([par_ref[s, 6:9], blank], axis=0)
        in_even = (count > s).astype(F32)
        both = jnp.concatenate([colours * in_even, colours * (1.0 - in_even)], axis=0)
        high = both.astype(BF16).astype(F32)
        return high, both - high

    @pl.loop(0, half // chunk)
    def _(step):
        start = pl.multiple_of(step * chunk, chunk)
        first = side * half + start
        for rows in parts:
            x_0, y_0 = place(first + rows.start + lax.broadcasted_iota(jnp.int32, (sub, size), 0))
            x_pos[rows] = x_0 - shift_x
            y_pos[rows] = y_0 - shift_y
        lane_ids = first + lax.broadcasted_iota(jnp.int32, (16, chunk), 1)
        carry = jnp.ones((chunk, 1), F32)
        image = jnp.zeros((32, chunk), F32)
        for s in range(segs):
            row = lambda r: par_ref[s, r : r + 1]
            mean_x, mean_y, opacity = row(0), row(1), row(5)
            k_a, k_b, k_c = (-0.5 * LOG2E) * row(2), (-LOG2E) * row(3), (-0.5 * LOG2E) * row(4)
            for rows in parts:
                dx = x_pos[rows] - mean_x
                dy = y_pos[rows] - mean_y
                alpha = opacity * jnp.exp2(dx * (k_a * dx + k_b * dy) + (k_c * dy) * dy)
                alphas[s, rows] = alpha
                high, low = split(jnp.log(1.0 - alpha))
                stage[rows, :size] = high
                stage[rows, size:] = low
            prefix = dot(stage[...], before)
            last = []
            for rows in parts:
                alpha = alphas[s, rows]
                trans = jnp.exp(prefix[rows]) * carry[rows]
                weight = alpha * trans
                weights[s, rows] = weight
                high, low = split(weight)
                w_pair[s, rows, :size] = high
                w_pair[s, rows, size:] = low
                last.append((trans - weight)[:, size - 1 :])
            carry = jnp.where(count == s + 1, 1.0, jnp.concatenate(last, axis=0))
            c_hi, c_lo = colour_rows(s)
            colours = jnp.concatenate([c_hi, c_lo], axis=0).astype(BF16)
            image = image + dot_nt(jnp.concatenate([colours, colours], axis=1), w_pair[s])
        in_tile = lax.broadcasted_iota(jnp.int32, (16, chunk), 0) < 8
        live = (lane_ids < jnp.where(in_tile, ray_even, ray_odd)).astype(F32)
        rendered = (image[:16] + image[16:]) * live
        cols = pl.ds(start, chunk)
        img_ref[0, :, cols] = rendered[:8]
        img_ref[1, :, cols] = rendered[8:]
        target = jnp.concatenate([tgt_ref[0, :, cols], tgt_ref[1, :, cols]], axis=0)
        residual = (rendered - target) * live
        r_hi = residual.astype(BF16).astype(F32)
        r_lo = residual - r_hi
        spread = jnp.concatenate([r_hi, r_lo, r_hi, jnp.zeros((LANES - 48, chunk), F32)], axis=0)
        spread = jnp.transpose(spread).astype(BF16)
        r_rows = jnp.concatenate([r_hi, r_lo], axis=0).astype(BF16)
        x_l, y_l = place(lane_ids[:1])
        squares = [x_l * x_l, x_l * y_l, y_l * y_l]
        sq_hi = [q.astype(BF16).astype(F32) for q in squares]
        none = jnp.zeros_like(x_l)
        features = [none + 1.0, x_l, y_l] + sq_hi + [none] * 5 + [q - h for q, h in zip(squares, sq_hi)] + [none] * 2
        features = jnp.concatenate(features, axis=0).astype(BF16)
        features = jnp.concatenate([features, features], axis=1)
        carry = jnp.zeros((chunk, 1), F32)
        for s in reversed(range(segs)):
            c_hi, c_lo = colour_rows(s)
            colours = jnp.concatenate([c_hi, c_hi, c_lo, jnp.zeros((LANES - 48, size), F32)], axis=0).astype(BF16)
            shaded = dot(spread, colours)
            for rows in parts:
                product = weights[s, rows] * shaded[rows]
                weights[s, rows] = product
                high, low = split(product)
                stage[rows, :size] = high
                stage[rows, size:] = low
            later = dot(stage[...], after)
            last = []
            for rows in parts:
                product = weights[s, rows]
                alpha = alphas[s, rows]
                tail = later[rows] + carry[rows]
                last.append((tail + product)[:, :1])
                rest = 1.0 - alpha
                inverse = pl.reciprocal(rest, approx=True)
                inverse = inverse * (2.0 - rest * inverse)
                high, low = split(product - alpha * inverse * tail)
                h_pair[rows] = high
                h_pair[slice(chunk + rows.start, chunk + rows.stop)] = low
            carry = jnp.where(count == s, 0.0, jnp.concatenate(last, axis=0))
            moments[s] += dot(features, h_pair[...])
            cgrads[s] += dot(r_rows, w_pair[s])

    for s in range(segs):
        row = lambda r: par_ref[s, r : r + 1]
        mean_x, mean_y = row(0) + shift_x, row(1) + shift_y
        m = [moments[s, k : k + 1] for k in range(3)] + [
            moments[s, k : k + 1] + moments[s, k + 8 : k + 9] for k in range(3, 6)
        ]
        along_x = m[1] - mean_x * m[0]
        along_y = m[2] - mean_y * m[0]
        square_x = m[3] - 2.0 * mean_x * m[1] + mean_x * mean_x * m[0]
        cross_xy = m[4] - mean_x * m[2] - mean_y * m[1] + mean_x * mean_y * m[0]
        square_y = m[5] - 2.0 * mean_y * m[2] + mean_y * mean_y * m[0]
        cg = cgrads[s, :16] + cgrads[s, 16:]
        cg = cg[:, :size] + cg[:, size:]
        grads = [
            row(2) * along_x + row(3) * along_y,
            row(3) * along_x + row(4) * along_y,
            -0.5 * square_x,
            -cross_xy,
            -0.5 * square_y,
            m[0] / row(5),
            jnp.where(count > s, cg[0:3], cg[8:11]),
        ]
        put(grad_ref, segs, s, jnp.concatenate(grads, axis=0))


def render(slots, params, infos, shift, halves):
    segs, rows, size = params.shape
    half = halves.shape[2]
    chunk = next(c for c in (384, 256, 128) if half % c == 0)
    vmem = pl.BlockSpec(memory_space=pltpu.VMEM)
    return pl.pallas_call(
        functools.partial(render_kernel, slots, chunk, 32),
        out_shape=(
            jax.ShapeDtypeStruct((packed_rows(segs, rows), size // 2), F32),
            jax.ShapeDtypeStruct(halves.shape, F32),
        ),
        in_specs=[vmem] * 4,
        out_specs=(vmem,) * 2,
        scratch_shapes=[
            pltpu.VMEM((segs, chunk, size), F32),
            pltpu.VMEM((segs, chunk, size), F32),
            pltpu.VMEM((segs, chunk, 2 * size), BF16),
            pltpu.VMEM((chunk, 2 * size), BF16),
            pltpu.VMEM((2 * chunk, size), BF16),
            pltpu.VMEM((chunk, size), F32),
            pltpu.VMEM((chunk, size), F32),
            pltpu.VMEM((segs, 16, size), F32),
            pltpu.VMEM((segs, 32, 2 * size), F32),
        ],
        compiler_params=pltpu.CompilerParams(vmem_limit_bytes=40 * 2**20),
        name="render_pair",
    )(params, infos, shift, halves)


def reduce_kernel(
    cells, views, slots, rows, grad_ref, infos, img_ref, out_ref, out_img, img_in, got, part, quarter, full,
    img_send, img_recv, seg_send, seg_recv, part_send, part_recv, full_send, full_recv,
):
    me = lax.axis_index("cell")
    view = lax.axis_index("view")
    side = me % 2
    per_block = out_ref.shape[0]
    share = per_block // views
    half = img_ref.shape[2]
    channels = out_img.shape[2]
    peers = cell_peers(cells, me)
    others = [(view + k) % views for k in range(1, views)]
    barrier = pltpu.get_barrier_semaphore()
    for cell, _, _, _ in peers:
        pl.semaphore_signal(barrier, inc=1, device_id={"cell": cell}, device_id_type=MESH)
    for other in others:
        pl.semaphore_signal(barrier, inc=1, device_id={"view": other}, device_id_type=MESH)
    pl.semaphore_wait(barrier, len(peers) + len(others))
    sends = []
    for n, (cell, _, _, theirs) in reversed(list(enumerate(peers))):
        copy = pltpu.make_async_remote_copy(
            grad_ref, got.at[theirs], seg_send.at[n], seg_recv.at[theirs],
            device_id={"cell": cell}, device_id_type=MESH,
        )
        copy.start()
        sends.append(copy)
    img_copy = pltpu.make_async_remote_copy(
        img_ref.at[1 - side], img_in, img_send, img_recv,
        device_id={"cell": peers[0][0]}, device_id_type=MESH,
    )
    img_copy.start()
    out_img[0, 0, :, pl.ds(pl.multiple_of(side * half, LANES), half)] = img_ref[side, :channels]
    ids, sums = [], []
    for pair in (0, -1, 1):
        for s, block in enumerate(pair_ids(infos[2 * pair + 2], infos[2 * pair + 3], slots)):
            ids.append(jnp.broadcast_to(block - me * per_block, out_ref.shape[1:]))
    for pair in (0, -1, 1):
        for n, (cell, distance, mine, _) in enumerate(peers):
            if distance == pair:
                pltpu.make_async_remote_copy(
                    grad_ref, got.at[mine], seg_send.at[n], seg_recv.at[mine],
                    device_id={"cell": cell}, device_id_type=MESH,
                ).wait_recv()
        if pair == 0:
            both = grad_ref[...] + got[3 - side]
        else:
            both = got[2 * pair + 2] + got[2 * pair + 3]
        sums += [take(both, slots + 1, s, rows) for s in range(slots + 1)]
    for b in range(per_block):
        total = jnp.zeros(out_ref.shape[1:], F32)
        for local, value in zip(ids, sums):
            total = total + jnp.where(local == b, value, 0.0)
        put(part.at[b // share], share, b % share, total)
    part_copies = []
    for k, other in enumerate(others):
        copy = pltpu.make_async_remote_copy(
            part.at[other], quarter.at[k], part_send.at[k], part_recv.at[k],
            device_id={"view": other}, device_id_type=MESH,
        )
        copy.start()
        part_copies.append(copy)
    total = part[view]
    for k, copy in enumerate(part_copies):
        copy.wait_recv()
        total = total + quarter[k]
    full[view] = total
    for k, other in enumerate(others):
        copy = pltpu.make_async_remote_copy(
            full.at[view], full.at[view], full_send.at[k], full_recv.at[k],
            device_id={"view": other}, device_id_type=MESH,
        )
        copy.start()
        sends.append(copy)
    img_copy.wait_recv()
    out_img[0, 0, :, pl.ds(pl.multiple_of((1 - side) * half, LANES), half)] = img_in[:channels]
    for k in range(views - 1):
        theirs = (view + views - 1 - k) % views
        pltpu.make_async_remote_copy(
            full.at[theirs], full.at[theirs], full_send.at[k], full_recv.at[k],
            device_id={"view": others[k]}, device_id_type=MESH,
        ).wait_recv()
    for b in range(per_block):
        out_ref[b] = take(full[b // share], share, b % share, rows)
    img_copy.wait_send()
    for copy in sends + part_copies:
        copy.wait_send()


def reduce_grads(cells, views, slots, shape, image_shape, grads, infos, images):
    vmem = pl.BlockSpec(memory_space=pltpu.VMEM)
    dma = pltpu.SemaphoreType.DMA
    share = shape[0] // views
    pack = (packed_rows(share, shape[1]), shape[2] // 2)
    return pl.pallas_call(
        functools.partial(reduce_kernel, cells, views, slots, shape[1]),
        out_shape=(
            jax.ShapeDtypeStruct(shape, F32),
            jax.ShapeDtypeStruct(image_shape, F32),
        ),
        in_specs=[vmem] * 3,
        out_specs=(vmem,) * 2,
        scratch_shapes=[
            pltpu.VMEM(images.shape[1:], F32),
            pltpu.VMEM((6,) + grads.shape, F32),
            pltpu.VMEM((views,) + pack, F32),
            pltpu.VMEM((views - 1,) + pack, F32),
            pltpu.VMEM((views,) + pack, F32),
            dma, dma, dma((5,)), dma((6,)),
            dma((views - 1,)), dma((views - 1,)), dma((views - 1,)), dma((views - 1,)),
        ],
        compiler_params=pltpu.CompilerParams(
            collective_id=1, has_side_effects=True, vmem_limit_bytes=24 * 2**20
        ),
        name="reduce_grads",
    )(grads, infos, images)


def shards(cells, views, gaussians, seg_count, seg_block, ray_count, camera_shift, target):
    slots = seg_block.shape[2]
    infos, params, targets = fetch(cells, seg_count, seg_block, ray_count, gaussians, target)
    grads, images = render(slots, params, infos, camera_shift, targets)
    gauss_grad, image = reduce_grads(cells, views, slots, gaussians.shape, target.shape, grads, infos, images)
    return (image, gauss_grad)


def solution(mesh):
    placed = (
        P("cell", None, None),
        P("view", "cell"),
        P("view", "cell", None),
        P("view", "cell"),
        P("view", None),
        P("view", "cell", None, None),
    )
    return jax.shard_map(
        functools.partial(shards, mesh.shape["cell"], mesh.shape["view"]),
        mesh=mesh,
        in_specs=placed,
        out_specs=(P("view", "cell", None, None), P("cell", None, None)),
        check_vma=False,
    )
```

time: 53 us -> 48.1 us (0.908)
  Pallas kernels: 46.6 us -> 42.1 us
  local copies, waits for them, and re-layouts: 2.16 us -> 3.81 us
  other arithmetic: 1.55 us -> 0 us
    pallas_call x2, Pallas kernels: 29.3 us -> 26.8 us  [the longest x1 13.9 us: reduce_grads(): pl.pallas_call(functools.partial(reduce_kernel, cells, views, slots, shap...]
    pallas_call x1, Pallas kernels: 17.4 us -> 15.3 us  [fetch(): pl.pallas_call(functools.partial(fetch_kernel, cells, slots), out_shape=(...]
    unnamed x7 -> x8, local copies, waits for them, and re-layouts: 2.13 us -> 3.81 us
    unnamed x1 -> x0, other arithmetic: 0.82 us -> none
    concatenate x1 -> x0, other arithmetic: 0.73 us -> none  [shards(): fields = jnp.concatenate([seg_count[0], seg_block[0, 0], ray_count[0]])]
where the time goes in v2:
time: 48.1 us; the launch traced here: 47.8 us
  Pallas kernels  42.1 us (88%)
  local copies, waits for them, and re-layouts  3.81 us (8%)
  between operations  1.97 us (4%)
    pallas_call x1, Pallas kernels, fetch(): pl.pallas_call(functools.partial(fetch_kernel, cells, slots), out_shape=(...  15.3 us
    pallas_call x1, Pallas kernels, reduce_grads(): pl.pallas_call(functools.partial(reduce_kernel, cells, views, slots, shap...  13.9 us
    pallas_call x1, Pallas kernels, render(): pl.pallas_call(functools.partial(render_kernel, slots, chunk, 32), out_sh...  12.8 us
    unnamed x8, local copies, waits for them, and re-layouts  3.81 us

profile of v2, /device:TPU:0, one launch (start us, length us, event | category | flops | bytes accessed | tf_op | source)
XLA Modules:
  0.0 47.8 jit_solution(16358956824208726938)
XLA Ops:
  1.9 0.8 %copy.9.tgt_ref = f32[1,1,3,2304]{3,2,1,0:T(4,128)S(1)} copy(f32[1,1,3,2304]{3,1,2,0:T(1,128)} %param.11) | data formatting | bytes 55296 | tf_op args[5]
  2.7 0.0 copy-start
  2.7 1.0 %copy.8.gauss_ref = f32[16,9,256]{2,1,0:T(8,128)S(1)} copy(f32[16,9,256]{2,0,1:T(8,128)} %param.6) | data formatting | bytes 294912 | tf_op args[0]
  3.7 0.0 copy-done
  3.7 15.3 %fetch_blocks.1 = (s32[6,8,128]{2,1,0:T(8,128)S(1)}, f32[4,9,256]{2,1,0:T(8,128)S(1)}, f32[2,8,1152]{2,1,0:T(8,128)S(1)}) custom-call(s32[1,1]{1,0:T(1,128)S(6)} %copy.12.count_ref, s32[1,1,3]{2,1,0:T(1,128)S(1)} %copy-done, s32[1,1]{1,0:T(1,128)S(6)} %copy.13.ray_ref, f32[16,9,256]{2,1,0:T(8,128)S(1)} %copy.8.gauss_ref, f32[1,1,3,2304]{3,2,1,0:T(4,128)S(1)} %copy.9.tgt_ref), custom_call_target="tpu_custom_call" | custom-call | tf_op jit(solution)/shard_map/fetch_blocks/pallas_call | solution.py:155
  19.0 0.0 copy-start.1
  19.0 0.6 %copy-done.1 = f32[1,2]{1,0:T(1,128)S(1)} copy-done((f32[1,2]{1,0:T(1,128)S(1)}, f32[1,2]{1,0:T(1,128)}, u32[]{:S(2)}) %copy-start.1) | copy-done | bytes 32
  19.7 12.8 %render_pair.1 = (f32[72,128]{1,0:T(8,128)S(1)}, f32[2,8,1152]{2,1,0:T(8,128)S(1)}) custom-call(f32[4,9,256]{2,1,0:T(8,128)S(1)} %get-tuple-element.9.par_ref, s32[6,8,128]{2,1,0:T(8,128)S(1)} %get-tuple-element.10.infos, f32[1,2]{1,0:T(1,128)S(1)} %copy-done.1, f32[2,8,1152]{2,1,0:T(8,128)S(1)} %get-tuple-element.11.tgt_ref), custom_call_target="tpu_custom_call" | custom-call | tf_op jit(solution)/shard_map/render_pair/pallas_call | solution.py:329
  32.5 13.9 %reduce_grads.1 = (f32[16,9,256]{2,1,0:T(8,128)S(1)}, f32[1,1,3,2304]{3,2,1,0:T(4,128)S(1)}) custom-call(f32[72,128]{1,0:T(8,128)S(1)} %get-tuple-element.12.grad_ref, s32[6,8,128]{2,1,0:T(8,128)S(1)} %get-tuple-element.10.infos, f32[2,8,1152]{2,1,0:T(8,128)S(1)} %get-tuple-element.13.img_ref), custom_call_target="tpu_custom_call" | custom-call | tf_op jit(solution)/shard_map/reduce_grads/pallas_call | solution.py:447
  46.4 0.6 %copy.10 = f32[1,1,3,2304]{3,1,2,0:T(1,128)} copy(f32[1,1,3,2304]{3,2,1,0:T(4,128)S(1)} %get-tuple-element.16) | data formatting | bytes 55296
  47.1 0.8 %copy.11 = f32[16,9,256]{2,0,1:T(8,128)} copy(f32[16,9,256]{2,1,0:T(8,128)S(1)} %get-tuple-element.17) | data formatting | bytes 294912
Async XLA Ops:
  2.7 1.0 %copy-start = (s32[1,1,3]{2,1,0:T(1,128)S(1)}, s32[1,1,3]{2,1,0:T(1,128)}, u32[]{:S(2)}) copy-start(s32[1,1,3]{2,1,0:T(1,128)} %block_ref.1) | copy-start | bytes 40
  19.0 0.7 %copy-start.1 = (f32[1,2]{1,0:T(1,128)S(1)}, f32[1,2]{1,0:T(1,128)}, u32[]{:S(2)}) copy-start(f32[1,2]{1,0:T(1,128)} %shift_ref.1) | copy-start | bytes 28
